TPU v7x, 512 devices: a whole 4x8x8 slice. The times are simulated.
512 devices in a mesh: row: 32 (over z, x), col: 16 (over y, core).
Axes of the slice: x: 4, y: 8, z: 8, core: 2. Of those that a mesh axis runs over, the one named last changes fastest.
Arguments:
- inv_diag: float32 [32, 4, 16, 8], P('row', None, 'col'), may hold values from -0.25 to 2, as said below
- panel: float32 [16, 8, 32, 3072], P('col', None, 'row'), may hold values from -2 to 2
- slab: float32 [32, 32, 16, 6144], P('row', None, 'col'), may hold values from -6 to 6
Outputs:
- updated: float32 [32, 32, 16, 6144], P('row', None, 'col')
Inputs may be any that keep to these rules, and one draw needn't show every extreme that they name: inv_diag holds a lower-triangular matrix with positive diagonal, entry (i, k) at [i % 32, i // 32, k % 16, k // 16].
All inputs are finite; a program needn't handle non-finite values.
Results may differ from a plain program's by a relative error of at most 0.00008.
Values sent between devices are 32-bit elements; how exact they have to be, the bound alone decides.
A program may use at most 64 MiB of HBM per device.

v0:
```python
import jax
import jax.numpy as jnp
from jax import lax
from jax.sharding import PartitionSpec as P

NB = 128
SR_DEV = 32


def spread(block, axis, owner):
    block = jnp.where(lax.axis_index(axis) == owner, block, jnp.zeros_like(block))
    return lax.psum(block, axis)


def body(inv_diag, panel, slab):
    rows_n = lax.axis_size("row")
    cols_n = lax.axis_size("col")
    flat = inv_diag.reshape(1, -1)
    pieces = lax.all_gather(flat, ("row", "col"), axis=0, tiled=True)
    inverse = (
        pieces.reshape(rows_n, cols_n, NB // rows_n, NB // cols_n)
        .transpose(2, 0, 3, 1)
        .reshape(NB, NB)
    )
    permuted = inverse.reshape(NB, NB // cols_n, cols_n).transpose(0, 2, 1).reshape(NB, NB)
    local_panel = panel[0, :, 0, :]
    column = lax.axis_index("col")
    group = rows_n // cols_n
    gathered = lax.all_gather(local_panel, "col", axis=0, tiled=True)
    solved = jnp.dot(
        permuted, gathered, precision=lax.Precision.HIGHEST, preferred_element_type=jnp.float32
    )
    row_side = solved[:, 0:SR_DEV]
    received = [spread(solved, "row", column + member * cols_n) for member in range(group)]
    col_side = jnp.stack(received, axis=2).reshape(NB, -1)
    update = lax.dot_general(
        row_side,
        col_side,
        (((0,), (0,)), ((), ())),
        precision=lax.Precision.HIGHEST,
        preferred_element_type=jnp.float32,
    )
    return (slab[0, :, 0, :] - update).reshape(slab.shape)


def solution(mesh):
    return jax.shard_map(
        body,
        mesh=mesh,
        in_specs=(
            P("row", None, "col", None),
            P("col", None, "row", None),
            P("row", None, "col", None),
        ),
        out_specs=P("row", None, "col", None),
        check_vma=False,
    )
```

profile of v0, /device:TPU:1, one launch (start us, length us, event | category | flops | bytes accessed | tf_op | source)
XLA Modules:
  0.0 265.5 jit_solution(4725986296383986515)
XLA Ops:
  6.5 0.0 all-gather.4.cloned.1.call-start
  6.5 0.7 all-gather.4.cloned.1.call-update
  7.3 0.0 all-reduce.3.cloned.1.call-start
  7.3 0.5 broadcast.9
  7.8 1.3 reduce.3
  9.2 0.1 reshape.21
  9.3 70.5 %all-gather.1 = f32[512,1,32]{2,1,0:T(1,128)S(1)} all-gather(f32[1,1,32]{2,1,0:T(1,128)S(1)} %reshape.21), channel_id=1, replica_groups=mesh['row'=32,'col'=16] {'row','col'}, dimensions={0}, use_global_device_ids=true | all-gather | bytes 65664 | tf_op jit(solution)/shard_map/all_gather | solution.py:19
  79.8 0.1 copy.10
  79.9 0.2 reshape.16
  80.1 0.2 copy.11
  80.3 0.2 reshape_reshape.3
  80.5 0.0 all-gather.4.cloned.1.call-done
  80.5 3.0 %fusion.1 = f32[128,3072]{1,0:T(8,128)S(1)} fusion(f32[1,128,1,3072]{3,2,0,1:T(1,128)} %all-gather.4.cloned.1.call-done, f32[128,16,8]{0,1,2:T(8,128)S(1)} %bitcast.25), kind=kOutput, calls=%fused_computation.3 | convolution fusion | flops 603979776 | bytes 3211264 | tf_op jit(solution)/shard_map/dot_general | solution.py:30
  83.5 0.0 copy-start
  83.5 2.1 select_bitcast_fusion.1
  85.6 0.0 copy-done
  85.6 0.0 all-reduce.3.cloned.1.call-update
  85.7 160.4 %all-reduce.3.cloned.1.call-done = (f32[128,3072,1]{1,0,2:T(8,128)}, f32[128,3072,1]{1,0,2:T(8,128)}) async-done(((f32[128,3072,1]{1,0,2:T(8,128)}, f32[128,3072,1]{1,0,2:T(8,128)}), (f32[128,3072,1]{1,0,2:T(8,128)}, f32[128,3072,1]{1,0,2:T(8,128)})) %all-reduce.3.cloned.1.call-update) | async-done | bytes 3145744 | tf_op jit(solution)/shard_map/psum | solution.py:12
  246.1 2.1 pad_maximum_fusion
  248.2 3.4 %copy.14 = f32[128,3072,2]{0,2,1:T(2,128)} copy(f32[128,3072,2]{1,0,2:T(8,128)S(1)} %pad_maximum_fusion) | data formatting | bytes 6291456 | tf_op jit(solution)/shard_map/stack | solution.py:35
  251.6 5.4 %fusion = f32[1,32,1,6144]{3,1,2,0:T(8,128)S(1)} fusion(f32[128,6144]{0,1:T(8,128)} %bitcast.23, f32[1,32,1,6144]{3,2,1,0:T(1,128)} %param.5, f32[128,3072]{1,0:T(8,128)} %copy-done), kind=kOutput, calls=%fused_computation.1 | convolution fusion | flops 302186496 | bytes 4784128 | tf_op jit(solution)/shard_map/dot_general | solution.py:36
  256.9 1.7 copy.15
Async XLA Ops:
  6.5 73.9 %all-gather.4.cloned.1.call-start = ((), (), s32[]{:S(2)}) async-start(), calls=%async_computation | async-start | bytes 1671168 | tf_op jit(solution)/shard_map/all_gather | solution.py:29
  7.3 238.8 %all-reduce.3.cloned.1.call-start = ((), (), s32[]{:S(2)}) async-start(), calls=%async_computation.1 | async-start | bytes 6291456 | tf_op jit(solution)/shard_map/psum | solution.py:12
  83.5 2.1 copy-start
Sparse Core Ops, SparseCore 0:
  9.5 47.2 all-gather.3
  85.8 160.2 all-reduce.2
where the time goes:
time: 269 us; the launch traced here: 265 us
  waiting for transfers between devices  161 us (60%)
  blocking collectives  70.5 us (26%)
  between operations  13.5 us (5%)
  matrix products  8.4 us (3%)
  local copies, waits for them, and re-layouts  6.36 us (2%)
  other arithmetic  5.55 us (2%)
    psum x1, waiting for transfers between devices, spread(): return lax.psum(block, axis)  160 us
    all_gather x1, blocking collectives, body(): pieces = lax.all_gather(flat, ('row', 'col'), axis=0, tiled=True)  70.5 us
    dot_general x1, matrix products, body(): lax.dot_general(row_side, col_side, (((0,), (0,)), ((), ())), precision=l...  5.39 us
  transfers between devices with their start and end apart: 2, of which 1 were waited for; matrix products, arithmetic and copies ran while one was open for 1% of the time, Pallas kernels for 0%

commit v1 on v0

v1 whole, which is shorter than its diff:
```python
import functools

import jax
import jax.numpy as jnp
from jax import lax
from jax.experimental import pallas as pl
from jax.experimental.pallas import tpu as pltpu
from jax.sharding import PartitionSpec as P

MESH = pl.DeviceIdType.MESH
NB = 128
NX, NY, NZ = 4, 8, 8
NC = 16
NR = 32
HALF = 1536
Q = 3
CW = HALF // Q
DZ = (1, -1, 3, -3)
F32 = jnp.float32
BF16 = jnp.bfloat16


def kernel(
    inv_ref,
    panel_ref,
    slab_ref,
    out_ref,
    inv_v,
    panel_lin,
    panel_t,
    slab_lin,
    slab_t,
    mine,
    gath,
    rowset,
    m_all,
    a_x,
    data,
    outb,
    urecv,
    out_lin,
    in_sem,
    out_sem,
    ga_send,
    ga_recv,
    gb_send,
    gb_recv,
    ax_send,
    ax_recv,
    sc_send,
    sc_recv,
    fw_send,
    ex_send,
    ex_recv,
):
    row = lax.axis_index("row")
    col = lax.axis_index("col")
    x = lax.rem(row, NX)
    z = lax.div(row, NX)
    y = lax.div(col, 2)
    core = lax.rem(col, 2)

    def dev(dx, dy, dz, dk):
        return (lax.rem(dz, NZ) * NX + lax.rem(dx, NX), lax.rem(dy, NY) * 2 + dk)

    def remote(src, dst, ss, rs, device):
        return pltpu.make_async_remote_copy(
            src_ref=src, dst_ref=dst, send_sem=ss, recv_sem=rs, device_id=device, device_id_type=MESH
        )

    my_member = lax.div(z, 4)
    to_x = jnp.where(my_member == 0, x, 3 - x)
    to_y = 2 * lax.rem(z, 4) + lax.div(x, 2)
    member = jnp.where(lax.div(x, 2) == lax.rem(y, 2), 0, 1)
    from_x = jnp.where(member == 0, x, 3 - x)
    from_z = lax.div(y, 2) + 4 * member
    to_core = lax.rem(from_x, 2)
    first = lax.rem(z + from_z, 2) == 1

    loads = [
        pltpu.make_async_copy(inv_ref, inv_v, in_sem.at[0]),
        pltpu.make_async_copy(panel_ref, panel_lin, in_sem.at[1]),
        pltpu.make_async_copy(slab_ref, slab_lin, in_sem.at[2]),
    ]
    for load in loads:
        load.start()

    barrier = pltpu.get_barrier_semaphore()

    def hello(device):
        pl.semaphore_signal(barrier, inc=1, device_id=device, device_id_type=MESH)

    @pl.when(first)
    def _():
        for i in range(NC):
            hello((from_z * NX + from_x, lax.rem(col + i, NC)))

    for i in range(1, NR):
        hello((lax.rem(row + i, NR), col))
    for i in range(1, NC):
        hello((row, lax.rem(col + i, NC)))
    for i in range(1, NX):
        hello(dev(x + i, y, z, 1 - core))

    lane = lax.broadcasted_iota(jnp.int32, (8, 128), 1)
    mine[...] = jnp.zeros_like(mine)
    loads[0].wait()
    for i in range(4):
        mine[i : i + 1, 0:8] = inv_v[0, i, :, :]
    placed = pltpu.roll(mine[0:8, :], col * 8, 1)
    mine[0:8, :] = placed
    loads[1].wait()
    head = panel_lin[pl.ds(0, 8, stride=24), :]
    mine[8:16, :] = pltpu.roll(jnp.where(lane < 32, head, 0.0), x * 32, 1)
    gath[pl.ds(col, 1)] = mine[...].reshape(1, 16, 128)
    perm = lax.div(lane, 2) + 64 * lax.rem(lane + my_member, 2)
    for b in range(24):
        tile = panel_lin[pl.ds(b, 8, stride=24), :]
        panel_t[:, b * 128 : (b + 1) * 128] = jnp.take_along_axis(tile, perm, axis=1)

    pl.semaphore_wait(barrier, 2 * len(DZ) + (NR - 1) + (NC - 1) + (NX - 1))

    for i in range(1, NC):
        remote(mine, gath.at[col], ga_send.at[0], ga_recv.at[0], (row, lax.rem(col + i, NC))).start()

    my_k = pl.multiple_of(col * 8, 8)
    scatter = []
    for q in range(Q):
        for d, dz in enumerate(DZ):
            for h in range(2):
                cp = remote(
                    panel_t.at[:, pl.ds(h * HALF + q * CW, CW)],
                    data.at[pl.ds(my_k, 8), pl.ds(q * CW, CW)],
                    sc_send.at[q, d, h],
                    sc_recv.at[col, q],
                    dev(to_x, to_y, z + dz + NZ, h),
                )
                cp.start()
                scatter.append(cp)

    loads[2].wait()
    for g in range(4):
        for b in range(48):
            slab_t[g * 8 : (g + 1) * 8, b * 128 : (b + 1) * 128] = slab_lin[pl.ds(g * 8 * 48 + b, 8, stride=48), :]

    pltpu.make_async_copy(gath.at[pl.ds(0, NC - 1)], gath.at[pl.ds(0, NC - 1)], ga_recv.at[0]).wait()
    rows = gath[0, 0:8, :]
    for i in range(1, NC):
        rows = rows + gath[i, 0:8, :]
    rowset[...] = rows
    my_r = pl.multiple_of(row * 8, 8)
    for i in range(1, NR):
        remote(rowset, m_all.at[pl.ds(my_r, 8)], gb_send.at[0], gb_recv.at[0], (lax.rem(row + i, NR), col)).start()
    m_all[pl.ds(my_r, 8), :] = rows
    for i in range(NC):
        a_x[x, i * 8 : (i + 1) * 8, :] = gath[i, 8:16, :]
    for i in range(1, NX):
        remote(a_x.at[x], a_x.at[x], ax_send.at[0], ax_recv.at[0], dev(x + i, y, z, core)).start()

    def arrived(c, q):
        piece = data.at[pl.ds(pl.multiple_of(c * 8, 8), 8), pl.ds(q * CW, CW)]
        pltpu.make_async_copy(piece, piece, sc_recv.at[c, q]).wait()
        return piece

    order = (0, 1, 7, 2, 6, 3, 5, 4)

    def forwards(q):
        out = []
        for dy in order:
            for k in range(2):
                c = lax.rem(y + dy, NY) * 2 + k
                piece = data.at[pl.ds(pl.multiple_of(c * 8, 8), 8), pl.ds(q * CW, CW)]
                out.append(
                    (c, remote(piece, piece, fw_send.at[c, q], sc_recv.at[c, q], dev(x, y, z + (1 if k == 0 else NZ - 1), core)))
                )
        return out

    for q in range(Q):

        @pl.when(first)
        def _():
            for c, cp in forwards(q):
                arrived(c, q)
                cp.start()

    pltpu.make_async_copy(a_x.at[pl.ds(0, 3)], a_x.at[pl.ds(0, 3)], ax_recv.at[0]).wait()
    heads = (a_x[0] + a_x[1] + a_x[2] + a_x[3]).T
    pltpu.make_async_copy(m_all.at[pl.ds(0, 8 * (NR - 1))], m_all.at[pl.ds(0, 8 * (NR - 1))], gb_recv.at[0]).wait()
    inverse = m_all[...]
    gram = jnp.dot(inverse.T, inverse, precision=lax.Precision.HIGHEST, preferred_element_type=F32)
    w = jnp.dot(heads, gram, precision=lax.Precision.HIGHEST, preferred_element_type=F32)
    wh = w.astype(BF16)
    wl = (w - wh.astype(F32)).astype(BF16)
    wcat = jnp.concatenate([wh, wl], axis=0)

    exchange = []
    for q in range(Q):

        @pl.when(jnp.logical_not(first))
        def _():
            for dy in order:
                for k in range(2):
                    arrived(lax.rem(y + dy, NY) * 2 + k, q)

        a = data[:, q * CW : (q + 1) * CW]
        ah = a.astype(BF16)
        al = (a - ah.astype(F32)).astype(BF16)
        both = jnp.dot(wcat, ah, preferred_element_type=F32)
        outb[q] = both[0:NB] + both[NB:] + jnp.dot(wh, al, preferred_element_type=F32)
        for i in range(1, NX):
            other = lax.rem(x + i, NX)
            cp = remote(
                outb.at[q, pl.ds(pl.multiple_of(other * 32, 32), 32)],
                urecv.at[member, core, q],
                ex_send.at[i, q],
                ex_recv.at[member, core, q],
                dev(x + i, y, z, to_core),
            )
            cp.start()
            exchange.append(cp)
        own = outb.at[q, pl.ds(pl.multiple_of(x * 32, 32), 32)]

        @pl.when(to_core == core)
        def _():
            pltpu.make_async_copy(own, urecv.at[member, core, q], ex_recv.at[member, core, q]).start()

        @pl.when(to_core != core)
        def _():
            remote(
                own, urecv.at[member, core, q], ex_send.at[0, q], ex_recv.at[member, core, q], dev(x, y, z, 1 - core)
            ).start()

    even = lax.rem(lane, 2) == 0
    swap = lane + 1 - 2 * lax.rem(lane, 2)
    for q in range(Q):
        for h in range(2):
            for m in range(2):
                slot = urecv.at[m, h, q]
                pltpu.make_async_copy(slot, slot, ex_recv.at[m, h, q]).wait()
            for t in range(CW // 128):
                b = 24 * h + 2 * (q * (CW // 128) + t)
                for g in range(4):
                    u0 = urecv[0, h, q, g * 8 : (g + 1) * 8, t * 128 : (t + 1) * 128]
                    u1 = urecv[1, h, q, g * 8 : (g + 1) * 8, t * 128 : (t + 1) * 128]
                    low = jnp.where(even, u0, u1)
                    high = jnp.take_along_axis(jnp.where(even, u1, u0), swap, axis=1)
                    s0 = slab_t[g * 8 : (g + 1) * 8, b * 128 : (b + 1) * 128]
                    s1 = slab_t[g * 8 : (g + 1) * 8, (b + 1) * 128 : (b + 2) * 128]
                    out_lin[pl.ds(g * 8 * 48 + b, 8, stride=48), :] = s0 - low
                    out_lin[pl.ds(g * 8 * 48 + b + 1, 8, stride=48), :] = s1 - high
    store = pltpu.make_async_copy(out_lin, out_ref, out_sem)
    store.start()

    for q in range(Q):

        @pl.when(first)
        def _():
            for _, cp in forwards(q):
                cp.wait_send()

        @pl.when(to_core != core)
        def _():
            own = outb.at[q, pl.ds(0, 32)]
            pltpu.make_async_copy(own, own, ex_send.at[0, q]).wait()

    for cp in scatter + exchange:
        cp.wait_send()
    pltpu.make_async_copy(gath.at[pl.ds(0, NC - 1)], gath.at[pl.ds(0, NC - 1)], ga_send.at[0]).wait()
    pltpu.make_async_copy(m_all.at[pl.ds(0, 8 * (NR - 1))], m_all.at[pl.ds(0, 8 * (NR - 1))], gb_send.at[0]).wait()
    pltpu.make_async_copy(a_x.at[pl.ds(0, 3)], a_x.at[pl.ds(0, 3)], ax_send.at[0]).wait()
    store.wait()


def body(inv_diag, panel, slab):
    dma = pltpu.SemaphoreType.DMA
    out = pl.pallas_call(
        kernel,
        out_shape=jax.ShapeDtypeStruct((1536, 128), F32),
        in_specs=[pl.BlockSpec(memory_space=pl.ANY)] * 3,
        out_specs=pl.BlockSpec(memory_space=pl.ANY),
        scratch_shapes=[
            pltpu.VMEM((1, 4, 1, 8), F32),
            pltpu.VMEM((192, 128), F32),
            pltpu.VMEM((8, 3072), F32),
            pltpu.VMEM((1536, 128), F32),
            pltpu.VMEM((32, 6144), F32),
            pltpu.VMEM((16, 128), F32),
            pltpu.VMEM((NC, 16, 128), F32),
            pltpu.VMEM((8, 128), F32),
            pltpu.VMEM((NR * 8, 128), F32),
            pltpu.VMEM((NX, NB, 128), F32),
            pltpu.VMEM((NB, HALF), F32),
            pltpu.VMEM((Q, NB, CW), F32),
            pltpu.VMEM((2, 2, Q, 32, CW), F32),
            pltpu.VMEM((1536, 128), F32),
            dma((3,)),
            dma,
            dma((1,)),
            dma((1,)),
            dma((1,)),
            dma((1,)),
            dma((1,)),
            dma((1,)),
            dma((Q, len(DZ), 2)),
            dma((NC, Q)),
            dma((NC, Q)),
            dma((NX, Q)),
            dma((2, 2, Q)),
        ],
        compiler_params=pltpu.CompilerParams(
            collective_id=0, has_side_effects=True, vmem_limit_bytes=40 * 2**20
        ),
        cost_estimate=pl.CostEstimate(flops=200_000_000, bytes_accessed=1_700_000, transcendentals=0),
        name="panel_step",
    )(inv_diag, panel.reshape(192, 128), slab.reshape(1536, 128))
    return out.reshape(slab.shape)


def solution(mesh):
    return jax.shard_map(
        body,
        mesh=mesh,
        in_specs=(
            P("row", None, "col", None),
            P("col", None, "row", None),
            P("row", None, "col", None),
        ),
        out_specs=P("row", None, "col", None),
        check_vma=False,
    )
```

time: 269 us -> 73.2 us (0.27); the launches traced: 265 us -> 72.6 us
  waiting for transfers between devices: 161 us -> 0 us
  blocking collectives: 70.5 us -> 0 us
  Pallas kernels: 0 us -> 69 us
  between operations: 13.5 us -> 0.01 us
  matrix products: 8.4 us -> 0 us
  other arithmetic: 5.55 us -> 0 us
  local copies, waits for them, and re-layouts: 6.36 us -> 3.59 us
    psum x1 -> x0, waiting for transfers between devices: 160 us -> none  [spread(): return lax.psum(block, axis)]
    all_gather x1 -> x0, blocking collectives: 70.5 us -> none  [body(): pieces = lax.all_gather(flat, ('row', 'col'), axis=0, tiled=True)]
    pallas_call x0 -> x1, Pallas kernels: none -> 69 us  [body(): pl.pallas_call(kernel, out_shape=jax.ShapeDtypeStruct((1536, 128), F32),...]
    dot_general x2 -> x0, matrix products: 8.4 us -> none  [the longest x1 5.39 us: body(): lax.dot_general(row_side, col_side, (((0,), (0,)), ((), ())), precision=l...]
    another operation x2 -> x0, other arithmetic: 4.21 us -> none  [body(): col_side = jnp.stack(received, axis=2).reshape(NB, -1)]
    another operation x2 -> x0, local copies, waits for them, and re-layouts: 3.54 us -> none  [the longest x1 3.38 us: body(): col_side = jnp.stack(received, axis=2).reshape(NB, -1)]
    unnamed x4 -> x7, local copies, waits for them, and re-layouts: 0.6 us -> 3.59 us
  transfers between devices with their start and end apart: 2 -> 0, of which waited for: 1 -> 0; matrix products, arithmetic and copies ran while one was open for 1% -> 0% of each run, Pallas kernels for 0% -> 0%
where the time goes in v1:
time: 73.2 us; the launch traced here: 72.6 us
  Pallas kernels  69 us (94%)
  local copies, waits for them, and re-layouts  3.59 us (5%)
    pallas_call x1, Pallas kernels, body(): pl.pallas_call(kernel, out_shape=jax.ShapeDtypeStruct((1536, 128), F32),...  69 us
    unnamed x7, local copies, waits for them, and re-layouts  3.59 us

profile of v1, /device:TPU:1, one launch (start us, length us, event | category | flops | bytes accessed | tf_op | source)
XLA Modules:
  0.0 72.6 jit_solution(6133463964495285215)
XLA Ops:
  0.0 0.0 copy-start.2
  0.0 0.7 copy-done.2
  0.7 0.0 copy-start
  0.7 1.1 %copy-done = f32[1,32,1,6144]{3,2,1,0:T(1,128)S(1)} copy-done((f32[1,32,1,6144]{3,2,1,0:T(1,128)S(1)}, f32[1,32,1,6144]{3,2,1,0:T(1,128)}, u32[]{:S(2)}) %copy-start) | copy-done | bytes 786456
  1.8 0.0 copy-start.1
  1.8 0.9 %copy-done.1 = f32[1,8,1,3072]{3,2,1,0:T(1,128)S(1)} copy-done((f32[1,8,1,3072]{3,2,1,0:T(1,128)S(1)}, f32[1,8,1,3072]{3,2,1,0:T(1,128)}, u32[]{:S(2)}) %copy-start.1) | copy-done | bytes 98328
  2.7 69.0 %panel_step.1 = f32[1536,128]{1,0:T(8,128)S(1)} custom-call(f32[1,4,1,8]{3,2,1,0:T(1,128)S(1)} %copy-done.2, f32[192,128]{1,0:T(8,128)S(1)} %bitcast.5, f32[1536,128]{1,0:T(8,128)S(1)} %bitcast.4), custom_call_target="tpu_custom_call" | custom-call | flops 200000000 | bytes 1700000 | tf_op jit(solution)/shard_map/panel_step/pallas_call | solution.py:276
  71.7 0.9 %copy.6 = f32[1,32,1,6144]{3,2,1,0:T(1,128)} copy(f32[1,32,1,6144]{3,2,1,0:T(1,128)S(1)} %bitcast.3) | data formatting | bytes 1572864
Async XLA Ops:
  0.0 0.7 copy-start.2
  0.7 1.1 %copy-start = (f32[1,32,1,6144]{3,2,1,0:T(1,128)S(1)}, f32[1,32,1,6144]{3,2,1,0:T(1,128)}, u32[]{:S(2)}) copy-start(f32[1,32,1,6144]{3,2,1,0:T(1,128)} %param.5) | copy-start | bytes 2359300
  1.8 0.9 %copy-start.1 = (f32[1,8,1,3072]{3,2,1,0:T(1,128)S(1)}, f32[1,8,1,3072]{3,2,1,0:T(1,128)}, u32[]{:S(2)}) copy-start(f32[1,8,1,3072]{3,2,1,0:T(1,128)} %param.4) | copy-start | bytes 294916

commit v2 on v1

v2 whole, which is shorter than its diff:
```python
import jax
import jax.numpy as jnp
from jax import lax
from jax.experimental import pallas as pl
from jax.experimental.pallas import tpu as pltpu
from jax.sharding import PartitionSpec as P

MESH = pl.DeviceIdType.MESH
NB = 128
NX, NY, NZ = 4, 8, 8
NC = 16
NR = 32
HALF = 1536
NQ = 4
CW = HALF // NQ
F32 = jnp.float32
BF16 = jnp.bfloat16
COLS = sorted(range(1, NC), key=lambda i: -min(i // 2, NY - i // 2))
ROWS = sorted(
    [(i, j) for i in range(NX) for j in range(NZ) if i or j],
    key=lambda s: -(min(s[0], NX - s[0]) + min(s[1], NZ - s[1])),
)
PLACE = [(c // 2 % 2) * 8 + c // 4 * 2 + c % 2 for c in range(NC)]


def kernel(
    inv_ref,
    panel_ref,
    slab_ref,
    out_ref,
    inv_v,
    panel_lin,
    panel_t,
    slab_lin,
    slab_t,
    mine,
    gath,
    rowset,
    m_all,
    a_x,
    data,
    outb,
    urecv,
    in_sem,
    ga_send,
    ga_recv,
    gb_send,
    gb_recv,
    ax_send,
    ax_recv,
    sc_send,
    blk_recv,
    ag_send,
    ex_send,
    ex_recv,
):
    row = lax.axis_index("row")
    col = lax.axis_index("col")
    x = lax.rem(row, NX)
    z = lax.div(row, NX)
    y = lax.div(col, 2)
    core = lax.rem(col, 2)

    def dev(dx, dy, dz, dk):
        return (lax.rem(dz, NZ) * NX + lax.rem(dx, NX), lax.rem(dy, NY) * 2 + dk)

    def remote(src, dst, ss, rs, device):
        return pltpu.make_async_remote_copy(
            src_ref=src, dst_ref=dst, send_sem=ss, recv_sem=rs, device_id=device, device_id_type=MESH
        )

    def settle(ref, sem):
        pltpu.make_async_copy(ref, ref, sem).wait()

    my_member = lax.div(z, 4)
    to_x = jnp.where(my_member == 0, x, 3 - x)
    to_y = 2 * lax.rem(z, 4) + lax.div(x, 2)
    member = jnp.where(lax.div(x, 2) == lax.rem(y, 2), 0, 1)
    from_x = jnp.where(member == 0, x, 3 - x)
    from_z = lax.div(y, 2) + 4 * member
    to_core = lax.rem(from_x, 2)
    side = lax.rem(y, 2)
    at_home = (to_x == x) & (to_y == y)
    stays = jnp.where(at_home & (side == lax.rem(z, 2)), 1, 0)

    loads = [
        pltpu.make_async_copy(inv_ref, inv_v, in_sem.at[0]),
        pltpu.make_async_copy(panel_ref, panel_lin, in_sem.at[1]),
        pltpu.make_async_copy(slab_ref, slab_lin, in_sem.at[2]),
    ]
    for load in loads:
        load.start()

    barrier = pltpu.get_barrier_semaphore()

    def hello(device):
        pl.semaphore_signal(barrier, inc=1, device_id=device, device_id_type=MESH)

    for u in range(4):
        for k in range(2):
            source = (from_z * NX + from_x, (2 * u + lax.rem(z, 2)) * 2 + k)

            @pl.when((source[0] != row) | (source[1] != col))
            def _():
                hello(source)

    for i, j in ROWS:
        hello(dev(x + i, y, z + j, core))
    for i in COLS:
        hello((row, lax.rem(col + i, NC)))
    for i in (2, 1, 3):
        hello(dev(x + i, y, z, 1 - core))

    lane = lax.broadcasted_iota(jnp.int32, (8, 128), 1)
    my_place = side * 8 + lax.div(y, 2) * 2 + core
    mine[...] = jnp.zeros_like(mine)
    loads[0].wait()
    for i in range(4):
        mine[i : i + 1, 0:8] = inv_v[0, i, :, :]
    placed = pltpu.roll(mine[0:8, :], my_place * 8, 1)
    mine[0:8, :] = placed
    loads[1].wait()
    head = panel_lin[pl.ds(0, 8, stride=24), :]
    mine[8:16, :] = pltpu.roll(jnp.where(lane < 32, head, 0.0), x * 32, 1)
    gath[pl.ds(col, 1)] = mine[...].reshape(1, 16, 128)
    perm = lax.div(lane, 2) + 64 * lax.rem(lane + my_member, 2)
    for b in range(24):
        tile = panel_lin[pl.ds(b, 8, stride=24), :]
        panel_t[:, b * 128 : (b + 1) * 128] = jnp.take_along_axis(tile, perm, axis=1)

    pl.semaphore_wait(barrier, 8 - stays + (NR - 1) + (NC - 1) + (NX - 1))

    for i in COLS:
        remote(mine, gath.at[col], ga_send.at[0], ga_recv.at[0], (row, lax.rem(col + i, NC))).start()

    my_u = lax.div(y, 2)
    my_rows = pl.ds(pl.multiple_of((my_u * 2 + core) * 8, 8), 8)

    def piece(q, h):
        return panel_t.at[:, pl.ds(h * HALF + q * CW, CW)]

    for q in range(NQ):
        s = 2 * q + side
        for h in range(2):
            here = (stays == 1) & (s == z) & (core == h)

            @pl.when(here)
            def _():
                pltpu.make_async_copy(piece(q, h), data.at[s, my_rows], blk_recv.at[s, my_u]).start()

            @pl.when(jnp.logical_not(here))
            def _():
                remote(
                    piece(q, h), data.at[s, my_rows], sc_send.at[q, h], blk_recv.at[s, my_u], dev(to_x, to_y, s, h)
                ).start()

    loads[2].wait()
    for g in range(4):
        for b in range(48):
            slab_t[g * 8 : (g + 1) * 8, b * 128 : (b + 1) * 128] = slab_lin[pl.ds(g * 8 * 48 + b, 8, stride=48), :]

    settle(gath.at[pl.ds(0, NC - 1)], ga_recv.at[0])
    rows = gath[0, 0:8, :]
    for i in range(1, NC):
        rows = rows + gath[i, 0:8, :]
    rowset[...] = rows
    my_r = pl.multiple_of(row * 8, 8)
    for i, j in ROWS:
        remote(rowset, m_all.at[pl.ds(my_r, 8)], gb_send.at[0], gb_recv.at[0], dev(x + i, y, z + j, core)).start()
    m_all[pl.ds(my_r, 8), :] = rows
    for i in range(NC):
        a_x[x, PLACE[i] * 8 : (PLACE[i] + 1) * 8, :] = gath[i, 8:16, :]
    for i in (2, 1, 3):
        remote(a_x.at[x], a_x.at[x], ax_send.at[0], ax_recv.at[0], dev(x + i, y, z, core)).start()

    odd = lax.rem(y + z, 2)
    subs = []
    for near, far in ((0, 1), (2, -1), (-2, 3), (4, -3)):
        yy = lax.rem(y + jnp.where(odd == 0, near, far) + NY, NY)
        subs.append(lax.div(yy, 2))

    def block(s, u):
        return data.at[s, pl.ds(pl.multiple_of(u * 16, 16), 16)]

    def pass_on(s, u, n, dz):
        return remote(block(s, u), block(s, u), ag_send.at[n], blk_recv.at[s, u], dev(x, y, z + dz + NZ, core))

    def have(s, u):
        settle(block(s, u), blk_recv.at[s, u])

    below = lax.rem(z + NZ - 2, NZ)
    above = lax.rem(z + 2, NZ)
    plan = []
    for i, u in enumerate(subs):
        plan.append((z, u, [2, -2, 1, -1]))
    for i, u in enumerate(subs):
        plan.append((below, u, [2, 1] if i in (0, 3) else [1]))
        plan.append((above, u, [-2, -1] if i in (1, 2) else [-1]))
    passed = []
    for s, u, steps in plan:
        have(s, u)
        for dz in steps:
            cp = pass_on(s, u, len(passed), dz)
            cp.start()
            passed.append(cp)

    settle(a_x.at[pl.ds(0, 3)], ax_recv.at[0])
    heads = (a_x[0] + a_x[1] + a_x[2] + a_x[3]).T
    settle(m_all.at[pl.ds(0, 8 * (NR - 1))], gb_recv.at[0])
    inverse = m_all[...]
    gram = jnp.dot(inverse.T, inverse, precision=lax.Precision.HIGHEST, preferred_element_type=F32)
    w = jnp.dot(heads, gram, precision=lax.Precision.HIGHEST, preferred_element_type=F32)
    wh = w.astype(BF16)
    wl = (w - wh.astype(F32)).astype(BF16)
    wcat = jnp.concatenate([wh, wl], axis=0)

    mine_q = lax.div(z, 2)
    lean = jnp.where(lax.rem(z, 2) == 0, 3, 1)
    chunks = [mine_q, lax.rem(mine_q + lean, NQ), lax.rem(mine_q + 4 - lean, NQ), lax.rem(mine_q + 2, NQ)]

    def late(s):
        return (s != z) & (s != below) & (s != above)

    exchange = []
    for n, q in enumerate(chunks):
        for half in range(2):
            s = 2 * q + half

            @pl.when(late(s))
            def _():
                for u in range(4):
                    have(s, u)

        a = jnp.concatenate([data[2 * q], data[2 * q + 1]], axis=0)
        ah = a.astype(BF16)
        al = (a - ah.astype(F32)).astype(BF16)
        both = jnp.dot(wcat, ah, preferred_element_type=F32)
        outb[n] = both[0:NB] + both[NB:] + jnp.dot(wh, al, preferred_element_type=F32)
        for i in (2, 1, 3):
            other = lax.rem(x + i, NX)
            cp = remote(
                outb.at[n, pl.ds(pl.multiple_of(other * 32, 32), 32)],
                urecv.at[member, core, n],
                ex_send.at[i, n],
                ex_recv.at[member, core, n],
                dev(x + i, y, z, to_core),
            )
            cp.start()
            exchange.append(cp)
        own = outb.at[n, pl.ds(pl.multiple_of(x * 32, 32), 32)]

        @pl.when(to_core == core)
        def _():
            pltpu.make_async_copy(own, urecv.at[member, core, n], ex_recv.at[member, core, n]).start()

        @pl.when(to_core != core)
        def _():
            remote(
                own, urecv.at[member, core, n], ex_send.at[0, n], ex_recv.at[member, core, n], dev(x, y, z, 1 - core)
            ).start()

    even = lax.rem(lane, 2) == 0
    swap = lane + 1 - 2 * lax.rem(lane, 2)
    for n, q in enumerate(chunks):
        for h in range(2):
            for m in range(2):
                settle(urecv.at[m, h, n], ex_recv.at[m, h, n])
            for t in range(CW // 128):
                b = 24 * h + 2 * (q * (CW // 128) + t)
                for g in range(4):
                    u0 = urecv[0, h, n, g * 8 : (g + 1) * 8, t * 128 : (t + 1) * 128]
                    u1 = urecv[1, h, n, g * 8 : (g + 1) * 8, t * 128 : (t + 1) * 128]
                    low = jnp.where(even, u0, u1)
                    high = jnp.take_along_axis(jnp.where(even, u1, u0), swap, axis=1)
                    s0 = slab_t[g * 8 : (g + 1) * 8, pl.ds(pl.multiple_of(b * 128, 128), 128)]
                    s1 = slab_t[g * 8 : (g + 1) * 8, pl.ds(pl.multiple_of(b * 128 + 128, 128), 128)]
                    out_ref[pl.ds(g * 8 * 48 + b, 8, stride=48), :] = s0 - low
                    out_ref[pl.ds(g * 8 * 48 + b + 1, 8, stride=48), :] = s1 - high

    for q in range(NQ):
        for h in range(2):
            here = (stays == 1) & (2 * q + side == z) & (core == h)

            @pl.when(jnp.logical_not(here))
            def _():
                settle(piece(q, h), sc_send.at[q, h])

    @pl.when(to_core != core)
    def _():
        for n in range(NQ):
            settle(outb.at[n, pl.ds(0, 32)], ex_send.at[0, n])

    for cp in passed + exchange:
        cp.wait_send()
    settle(gath.at[pl.ds(0, NC - 1)], ga_send.at[0])
    settle(m_all.at[pl.ds(0, 8 * (NR - 1))], gb_send.at[0])
    settle(a_x.at[pl.ds(0, 3)], ax_send.at[0])


def body(inv_diag, panel, slab):
    dma = pltpu.SemaphoreType.DMA
    out = pl.pallas_call(
        kernel,
        out_shape=jax.ShapeDtypeStruct((1536, 128), F32),
        in_specs=[pl.BlockSpec(memory_space=pl.ANY)] * 3,
        out_specs=pl.BlockSpec(memory_space=pltpu.VMEM),
        scratch_shapes=[
            pltpu.VMEM((1, 4, 1, 8), F32),
            pltpu.VMEM((192, 128), F32),
            pltpu.VMEM((8, 3072), F32),
            pltpu.VMEM((1536, 128), F32),
            pltpu.VMEM((32, 6144), F32),
            pltpu.VMEM((16, 128), F32),
            pltpu.VMEM((NC, 16, 128), F32),
            pltpu.VMEM((8, 128), F32),
            pltpu.VMEM((NR * 8, 128), F32),
            pltpu.VMEM((NX, NB, 128), F32),
            pltpu.VMEM((8, 64, CW), F32),
            pltpu.VMEM((NQ, NB, CW), F32),
            pltpu.VMEM((2, 2, NQ, 32, CW), F32),
            dma((3,)),
            dma((1,)),
            dma((1,)),
            dma((1,)),
            dma((1,)),
            dma((1,)),
            dma((1,)),
            dma((NQ, 2)),
            dma((8, 4)),
            dma((28,)),
            dma((NX, NQ)),
            dma((2, 2, NQ)),
        ],
        compiler_params=pltpu.CompilerParams(
            collective_id=0, has_side_effects=True, vmem_limit_bytes=60 * 2**20
        ),
        cost_estimate=pl.CostEstimate(flops=200_000_000, bytes_accessed=1_700_000, transcendentals=0),
        name="panel_step",
    )(inv_diag, panel.reshape(192, 128), slab.reshape(1536, 128))
    return out.reshape(slab.shape)


def solution(mesh):
    return jax.shard_map(
        body,
        mesh=mesh,
        in_specs=(
            P("row", None, "col", None),
            P("col", None, "row", None),
            P("row", None, "col", None),
        ),
        out_specs=P("row", None, "col", None),
        check_vma=False,
    )
```

time: 73.2 us -> 53.8 us (0.73)
  the two profiles are of different devices: /device:TPU:1 before, /device:TPU:41 now
where the time goes in v2:
time: 53.8 us; the launch traced here: 53.7 us
  Pallas kernels  51.6 us (96%)
  local copies, waits for them, and re-layouts  2.06 us (4%)
    pallas_call x1, Pallas kernels, body(): pl.pallas_call(kernel, out_shape=jax.ShapeDtypeStruct((1536, 128), F32),...  51.6 us
    unnamed x1, local copies, waits for them, and re-layouts  2.06 us

profile of v2, /device:TPU:41, one launch (start us, length us, event | category | flops | bytes accessed | tf_op | source)
XLA Modules:
  0.0 53.7 jit_solution(16750997740091708133)
XLA Ops:
  0.0 51.6 %panel_step.1 = f32[1536,128]{1,0:T(8,128)} custom-call(f32[1,4,1,8]{3,2,1,0:T(1,128)} %inv_ref.1, f32[192,128]{1,0:T(8,128)} %bitcast.5, f32[1536,128]{1,0:T(8,128)} %bitcast.4), custom_call_target="tpu_custom_call" | custom-call | flops 200000000 | bytes 1700000 | tf_op jit(solution)/shard_map/panel_step/pallas_call | solution.py:302
  51.6 2.1 %copy.6 = f32[1,32,1,6144]{3,2,1,0:T(1,128)} copy(f32[1,32,1,6144]{3,2,1,0:T(1,128)} %bitcast.3) | data formatting | bytes 1572864

commit v3 on v2

--- a/solution.py
+++ b/solution.py
@@ -13,6 +13,8 @@
 HALF = 1536
 NQ = 4
 CW = HALF // NQ
+W_AT = 8
+FIRST_AT = 10
 F32 = jnp.float32
 BF16 = jnp.bfloat16
 COLS = sorted(range(1, NC), key=lambda i: -min(i // 2, NY - i // 2))
@@ -38,9 +40,11 @@
     rowset,
     m_all,
     a_x,
+    stage,
     data,
     outb,
     urecv,
+    wcat,
     in_sem,
     ga_send,
     ga_recv,
@@ -48,6 +52,8 @@
     gb_recv,
     ax_send,
     ax_recv,
+    za_send,
+    za_recv,
     sc_send,
     blk_recv,
     ag_send,
@@ -73,15 +79,12 @@
         pltpu.make_async_copy(ref, ref, sem).wait()
 
     my_member = lax.div(z, 4)
-    to_x = jnp.where(my_member == 0, x, 3 - x)
-    to_y = 2 * lax.rem(z, 4) + lax.div(x, 2)
     member = jnp.where(lax.div(x, 2) == lax.rem(y, 2), 0, 1)
     from_x = jnp.where(member == 0, x, 3 - x)
     from_z = lax.div(y, 2) + 4 * member
     to_core = lax.rem(from_x, 2)
     side = lax.rem(y, 2)
-    at_home = (to_x == x) & (to_y == y)
-    stays = jnp.where(at_home & (side == lax.rem(z, 2)), 1, 0)
+    active = side == lax.rem(z, 2)
 
     loads = [
         pltpu.make_async_copy(inv_ref, inv_v, in_sem.at[0]),
@@ -96,9 +99,10 @@
     def hello(device):
         pl.semaphore_signal(barrier, inc=1, device_id=device, device_id_type=MESH)
 
+    own_too = jnp.where((from_x == x) & active, 1, 0)
     for u in range(4):
         for k in range(2):
-            source = (from_z * NX + from_x, (2 * u + lax.rem(z, 2)) * 2 + k)
+            source = (z * NX + from_x, (2 * u + lax.rem(z, 2)) * 2 + k)
 
             @pl.when((source[0] != row) | (source[1] != col))
             def _():
@@ -124,40 +128,61 @@
     mine[8:16, :] = pltpu.roll(jnp.where(lane < 32, head, 0.0), x * 32, 1)
     gath[pl.ds(col, 1)] = mine[...].reshape(1, 16, 128)
     perm = lax.div(lane, 2) + 64 * lax.rem(lane + my_member, 2)
-    for b in range(24):
-        tile = panel_lin[pl.ds(b, 8, stride=24), :]
-        panel_t[:, b * 128 : (b + 1) * 128] = jnp.take_along_axis(tile, perm, axis=1)
-
-    pl.semaphore_wait(barrier, 8 - stays + (NR - 1) + (NC - 1) + (NX - 1))
+    for q in range(NQ):
+        for h in range(2):
+            for t in range(3):
+                tile = panel_lin[pl.ds(12 * h + 3 * q + t, 8, stride=24), :]
+                panel_t[q, :, (3 * h + t) * 128 : (3 * h + t + 1) * 128] = jnp.take_along_axis(tile, perm, axis=1)
+
+    pl.semaphore_wait(barrier, jnp.where(active, 16, 0) - own_too + (NR - 1) + (NC - 1) + (NX - 1))
+
+    for q in range(NQ):
+        zq = 2 * q + side
+
+        @pl.when(zq == z)
+        def _():
+            pltpu.make_async_copy(panel_t.at[q], stage.at[z], za_recv.at[z]).start()
+
+        @pl.when(zq != z)
+        def _():
+            remote(panel_t.at[q], stage.at[z], za_send.at[q], za_recv.at[z], dev(x, y, zq, core)).start()
 
     for i in COLS:
         remote(mine, gath.at[col], ga_send.at[0], ga_recv.at[0], (row, lax.rem(col + i, NC))).start()
-
-    my_u = lax.div(y, 2)
-    my_rows = pl.ds(pl.multiple_of((my_u * 2 + core) * 8, 8), 8)
-
-    def piece(q, h):
-        return panel_t.at[:, pl.ds(h * HALF + q * CW, CW)]
-
-    for q in range(NQ):
-        s = 2 * q + side
-        for h in range(2):
-            here = (stays == 1) & (s == z) & (core == h)
-
-            @pl.when(here)
-            def _():
-                pltpu.make_async_copy(piece(q, h), data.at[s, my_rows], blk_recv.at[s, my_u]).start()
-
-            @pl.when(jnp.logical_not(here))
-            def _():
-                remote(
-                    piece(q, h), data.at[s, my_rows], sc_send.at[q, h], blk_recv.at[s, my_u], dev(to_x, to_y, s, h)
-                ).start()
 
     loads[2].wait()
     for g in range(4):
         for b in range(48):
             slab_t[g * 8 : (g + 1) * 8, b * 128 : (b + 1) * 128] = slab_lin[pl.ds(g * 8 * 48 + b, 8, stride=48), :]
+
+    my_u = lax.div(y, 2)
+    my_rows = pl.ds(pl.multiple_of((my_u * 2 + core) * 8, 8), 8)
+
+    def hop(n, h):
+        src = lax.rem(z + n, NZ)
+        goes_x = jnp.where(src < 4, x, 3 - x)
+        goes_y = 2 * lax.rem(src, 4) + lax.div(x, 2)
+        piece = stage.at[src, :, pl.ds(h * CW, CW)]
+        here = (goes_x == x) & (goes_y == y) & (core == h)
+        return src, goes_x, goes_y, piece, here
+
+    @pl.when(active)
+    def _():
+        for n in (0, 1, 7, 2, 6, 3, 5, 4):
+            src = hop(n, 0)[0]
+            settle(stage.at[src], za_recv.at[src])
+            for h in range(2):
+                _, goes_x, goes_y, piece, here = hop(n, h)
+
+                @pl.when(here)
+                def _():
+                    pltpu.make_async_copy(piece, data.at[z, my_rows], blk_recv.at[z, my_u]).start()
+
+                @pl.when(jnp.logical_not(here))
+                def _():
+                    remote(
+                        piece, data.at[z, my_rows], sc_send.at[n, h], blk_recv.at[z, my_u], dev(goes_x, goes_y, z, h)
+                    ).start()
 
     settle(gath.at[pl.ds(0, NC - 1)], ga_recv.at[0])
     rows = gath[0, 0:8, :]
@@ -196,37 +221,29 @@
     for i, u in enumerate(subs):
         plan.append((below, u, [2, 1] if i in (0, 3) else [1]))
         plan.append((above, u, [-2, -1] if i in (1, 2) else [-1]))
-    passed = []
-    for s, u, steps in plan:
-        have(s, u)
-        for dz in steps:
-            cp = pass_on(s, u, len(passed), dz)
-            cp.start()
-            passed.append(cp)
-
-    settle(a_x.at[pl.ds(0, 3)], ax_recv.at[0])
-    heads = (a_x[0] + a_x[1] + a_x[2] + a_x[3]).T
-    settle(m_all.at[pl.ds(0, 8 * (NR - 1))], gb_recv.at[0])
-    inverse = m_all[...]
-    gram = jnp.dot(inverse.T, inverse, precision=lax.Precision.HIGHEST, preferred_element_type=F32)
-    w = jnp.dot(heads, gram, precision=lax.Precision.HIGHEST, preferred_element_type=F32)
-    wh = w.astype(BF16)
-    wl = (w - wh.astype(F32)).astype(BF16)
-    wcat = jnp.concatenate([wh, wl], axis=0)
+
+    def weights():
+        settle(a_x.at[pl.ds(0, 3)], ax_recv.at[0])
+        heads = (a_x[0] + a_x[1] + a_x[2] + a_x[3]).T
+        settle(m_all.at[pl.ds(0, 8 * (NR - 1))], gb_recv.at[0])
+        inverse = m_all[...]
+        gram = jnp.dot(inverse.T, inverse, precision=lax.Precision.HIGHEST, preferred_element_type=F32)
+        w = jnp.dot(heads, gram, precision=lax.Precision.HIGHEST, preferred_element_type=F32)
+        wh = w.astype(BF16)
+        wcat[0:NB] = wh
+        wcat[NB:] = (w - wh.astype(F32)).astype(BF16)
 
     mine_q = lax.div(z, 2)
     lean = jnp.where(lax.rem(z, 2) == 0, 3, 1)
     chunks = [mine_q, lax.rem(mine_q + lean, NQ), lax.rem(mine_q + 4 - lean, NQ), lax.rem(mine_q + 2, NQ)]
-
-    def late(s):
-        return (s != z) & (s != below) & (s != above)
-
     exchange = []
-    for n, q in enumerate(chunks):
+
+    def chunk(n):
+        q = chunks[n]
         for half in range(2):
             s = 2 * q + half
 
-            @pl.when(late(s))
+            @pl.when((s != z) & (s != below) & (s != above))
             def _():
                 for u in range(4):
                     have(s, u)
@@ -234,8 +251,8 @@
         a = jnp.concatenate([data[2 * q], data[2 * q + 1]], axis=0)
         ah = a.astype(BF16)
         al = (a - ah.astype(F32)).astype(BF16)
-        both = jnp.dot(wcat, ah, preferred_element_type=F32)
-        outb[n] = both[0:NB] + both[NB:] + jnp.dot(wh, al, preferred_element_type=F32)
+        both = jnp.dot(wcat[...], ah, preferred_element_type=F32)
+        outb[n] = both[0:NB] + both[NB:] + jnp.dot(wcat[0:NB], al, preferred_element_type=F32)
         for i in (2, 1, 3):
             other = lax.rem(x + i, NX)
             cp = remote(
@@ -258,6 +275,22 @@
             remote(
                 own, urecv.at[member, core, n], ex_send.at[0, n], ex_recv.at[member, core, n], dev(x, y, z, 1 - core)
             ).start()
+
+    passed = []
+    for step, (s, u, steps) in enumerate(plan):
+        if step == W_AT:
+            weights()
+        if step == FIRST_AT:
+            chunk(0)
+        have(s, u)
+        for dz in steps:
+            cp = pass_on(s, u, len(passed), dz)
+            cp.start()
+            passed.append(cp)
+    if W_AT >= len(plan):
+        weights()
+    for n in range(1 if FIRST_AT < len(plan) else 0, NQ):
+        chunk(n)
 
     even = lax.rem(lane, 2) == 0
     swap = lane + 1 - 2 * lax.rem(lane, 2)
@@ -278,12 +311,20 @@
                     out_ref[pl.ds(g * 8 * 48 + b + 1, 8, stride=48), :] = s1 - high
 
     for q in range(NQ):
-        for h in range(2):
-            here = (stays == 1) & (2 * q + side == z) & (core == h)
-
-            @pl.when(jnp.logical_not(here))
-            def _():
-                settle(piece(q, h), sc_send.at[q, h])
+
+        @pl.when(2 * q + side != z)
+        def _():
+            settle(panel_t.at[q], za_send.at[q])
+
+    @pl.when(active)
+    def _():
+        for n in range(8):
+            for h in range(2):
+                _, _, _, piece, here = hop(n, h)
+
+                @pl.when(jnp.logical_not(here))
+                def _():
+                    settle(piece, sc_send.at[n, h])
 
     @pl.when(to_core != core)
     def _():
@@ -307,7 +348,7 @@
         scratch_shapes=[
             pltpu.VMEM((1, 4, 1, 8), F32),
             pltpu.VMEM((192, 128), F32),
-            pltpu.VMEM((8, 3072), F32),
+            pltpu.VMEM((NQ, 8, 2 * CW), F32),
             pltpu.VMEM((1536, 128), F32),
             pltpu.VMEM((32, 6144), F32),
             pltpu.VMEM((16, 128), F32),
@@ -315,9 +356,11 @@
             pltpu.VMEM((8, 128), F32),
             pltpu.VMEM((NR * 8, 128), F32),
             pltpu.VMEM((NX, NB, 128), F32),
+            pltpu.VMEM((NZ, 8, 2 * CW), F32),
             pltpu.VMEM((8, 64, CW), F32),
             pltpu.VMEM((NQ, NB, CW), F32),
             pltpu.VMEM((2, 2, NQ, 32, CW), F32),
+            pltpu.VMEM((2 * NB, NB), BF16),
             dma((3,)),
             dma((1,)),
             dma((1,)),
@@ -325,7 +368,9 @@
             dma((1,)),
             dma((1,)),
             dma((1,)),
-            dma((NQ, 2)),
+            dma((NQ,)),
+            dma((NZ,)),
+            dma((NZ, 2)),
             dma((8, 4)),
             dma((28,)),
             dma((NX, NQ)),

time: 53.8 us -> 48.7 us (0.905)
  the two profiles are of different devices: /device:TPU:41 before, /device:TPU:1 now
where the time goes in v3:
time: 48.7 us; the launch traced here: 48.2 us
  Pallas kernels  46.1 us (95%)
  local copies, waits for them, and re-layouts  2.06 us (4%)
    pallas_call x1, Pallas kernels, body(): pl.pallas_call(kernel, out_shape=jax.ShapeDtypeStruct((1536, 128), F32),...  46.1 us
    unnamed x1, local copies, waits for them, and re-layouts  2.06 us

profile of v3, /device:TPU:1, one launch (start us, length us, event | category | flops | bytes accessed | tf_op | source)
XLA Modules:
  0.0 48.2 jit_solution(13088208191759999200)
XLA Ops:
  0.0 46.1 %panel_step.1 = f32[1536,128]{1,0:T(8,128)} custom-call(f32[1,4,1,8]{3,2,1,0:T(1,128)} %inv_ref.1, f32[192,128]{1,0:T(8,128)} %bitcast.5, f32[1536,128]{1,0:T(8,128)} %bitcast.4), custom_call_target="tpu_custom_call" | custom-call | flops 200000000 | bytes 1700000 | tf_op jit(solution)/shard_map/panel_step/pallas_call | solution.py:343
  46.1 2.1 %copy.6 = f32[1,32,1,6144]{3,2,1,0:T(1,128)} copy(f32[1,32,1,6144]{3,2,1,0:T(1,128)} %bitcast.3) | data formatting | bytes 1572864

commit v4 on v3

v4 whole, which is shorter than its diff:
```python
import jax
import jax.numpy as jnp
from jax import lax
from jax.experimental import pallas as pl
from jax.experimental.pallas import tpu as pltpu
from jax.sharding import PartitionSpec as P

MESH = pl.DeviceIdType.MESH
NB = 128
NX, NY, NZ = 4, 8, 8
NC = 16
HALF = 1536
NQ = 4
CW = HALF // NQ
F32 = jnp.float32
BF16 = jnp.bfloat16
COLS = sorted(range(1, NC), key=lambda i: -min(i // 2, NY - i // 2))
ZS = (4, 3, 5, 2, 6, 1, 7)
PLACE = [c % 2 * 8 + c // 2 for c in range(NC)]
ORDER = (
    "h0", "h1", "h7", "h2", "h6", "h3", "h5", "a", "h4", "A0", "H", "A1",
    "b", "A2", "A3", "B0", "W", "B1", "C0", "B2", "B3", "C1", "C2", "C3",
)


def kernel(
    inv_ref,
    panel_ref,
    slab_ref,
    out_ref,
    inv_v,
    panel_lin,
    panel_t,
    slab_lin,
    slab_t,
    mine,
    mine_head,
    gath,
    gath_head,
    m_z,
    m_x,
    a_x,
    stage,
    data,
    outb,
    urecv,
    wcat,
    in_sem,
    ga_send,
    ga_recv,
    gh_send,
    gh_recv,
    gb_send,
    gb_recv,
    gc_send,
    gc_recv,
    ax_send,
    ax_recv,
    za_send,
    za_recv,
    sc_send,
    blk_recv,
    ag_send,
    ex_send,
    ex_recv,
):
    row = lax.axis_index("row")
    col = lax.axis_index("col")
    x = lax.rem(row, NX)
    z = lax.div(row, NX)
    y = lax.div(col, 2)
    core = lax.rem(col, 2)

    def dev(dx, dy, dz, dk):
        return (lax.rem(dz, NZ) * NX + lax.rem(dx, NX), lax.rem(dy, NY) * 2 + dk)

    def remote(src, dst, ss, rs, device):
        return pltpu.make_async_remote_copy(
            src_ref=src, dst_ref=dst, send_sem=ss, recv_sem=rs, device_id=device, device_id_type=MESH
        )

    def settle(ref, sem):
        pltpu.make_async_copy(ref, ref, sem).wait()

    my_member = lax.div(z, 4)
    member = jnp.where(lax.div(x, 2) == lax.rem(y, 2), 0, 1)
    from_x = jnp.where(member == 0, x, 3 - x)
    from_z = lax.div(y, 2) + 4 * member
    to_core = lax.rem(from_x, 2)
    active = core == lax.rem(z, 2)

    loads = [
        pltpu.make_async_copy(inv_ref, inv_v, in_sem.at[0]),
        pltpu.make_async_copy(panel_ref, panel_lin, in_sem.at[1]),
        pltpu.make_async_copy(slab_ref, slab_lin, in_sem.at[2]),
    ]
    for load in loads:
        load.start()

    barrier = pltpu.get_barrier_semaphore()

    def hello(device):
        pl.semaphore_signal(barrier, inc=1, device_id=device, device_id_type=MESH)

    for i in ZS:
        hello(dev(x, y, z + i, core))

    @pl.when(member == 1)
    def _():
        for i in (4, 3, 5, 2, 6, 1, 7, 0):
            hello(dev(from_x, y + i, z, lax.rem(z, 2)))

    for i in COLS:
        hello((row, lax.rem(col + i, NC)))
    for i in (2, 1, 3):
        for k in range(2):
            hello(dev(x + i, y, z, k))

    lane = lax.broadcasted_iota(jnp.int32, (8, 128), 1)
    mine[...] = jnp.zeros_like(mine)
    loads[0].wait()
    for i in range(4):
        mine[i : i + 1, 0:8] = inv_v[0, i, :, :]
    placed = pltpu.roll(pltpu.roll(mine[...], (core * 8 + y) * 8, 1), 4 * lax.rem(z, 2), 0)
    mine[...] = placed
    loads[1].wait()
    head = panel_lin[pl.ds(0, 8, stride=24), :]
    mine_head[...] = pltpu.roll(jnp.where(lane < 32, head, 0.0), x * 32, 1)
    gath_head[pl.ds(col, 1)] = mine_head[...].reshape(1, 8, 128)
    gath[pl.ds(col, 1)] = mine[...].reshape(1, 8, 128)
    perm = lax.div(lane, 2) + 64 * lax.rem(lane + my_member, 2)
    for q in range(NQ):
        for h in range(2):
            for t in range(3):
                tile = panel_lin[pl.ds(12 * h + 3 * q + t, 8, stride=24), :]
                panel_t[q, :, (3 * h + t) * 128 : (3 * h + t + 1) * 128] = jnp.take_along_axis(tile, perm, axis=1)

    pl.semaphore_wait(barrier, (NC - 1) + (NZ - 1) + 2 * (NX - 1) + jnp.where(active, 8, 0))

    for near, far in ((0, 1), (2, -1), (-2, 3), (4, -3)):
        zq = lax.rem(z + jnp.where(active, near, far) + NZ, NZ)
        piece_z = panel_t.at[lax.div(zq, 2)]

        @pl.when(zq == z)
        def _():
            pltpu.make_async_copy(piece_z, stage.at[z], za_recv.at[z]).start()

        @pl.when(zq != z)
        def _():
            remote(piece_z, stage.at[z], za_send.at[0], za_recv.at[z], dev(x, y, zq, core)).start()

    for i in COLS:
        remote(mine, gath.at[col], ga_send.at[0], ga_recv.at[0], (row, lax.rem(col + i, NC))).start()
    for i in COLS:
        remote(
            mine_head, gath_head.at[col], gh_send.at[0], gh_recv.at[0], (row, lax.rem(col + i, NC))
        ).start()

    loads[2].wait()
    for g in range(4):
        for b in range(48):
            slab_t[g * 8 : (g + 1) * 8, b * 128 : (b + 1) * 128] = slab_lin[pl.ds(g * 8 * 48 + b, 8, stride=48), :]

    my_rows = pl.ds(pl.multiple_of(y * 8, 8), 8)

    def hop(n):
        src = lax.rem(z + n, NZ)
        goes_x = jnp.where(src < 4, x, 3 - x)
        goes_y = 2 * lax.rem(src, 4) + lax.div(x, 2)
        at_home = (goes_x == x) & (goes_y == y)
        arrive = blk_recv.at[z, lax.div(y, 2)]

        @pl.when(active)
        def _():
            settle(stage.at[src], za_recv.at[src])
            for h in range(2):
                piece = stage.at[src, :, pl.ds(h * CW, CW)]

                @pl.when(at_home & (core == h))
                def _():
                    pltpu.make_async_copy(piece, data.at[z, my_rows], arrive).start()

                @pl.when(jnp.logical_not(at_home & (core == h)))
                def _():
                    remote(piece, data.at[z, my_rows], sc_send.at[0], arrive, dev(goes_x, goes_y, z, h)).start()

    def inv_along_z():
        settle(gath.at[pl.ds(0, NC - 1)], ga_recv.at[0])
        rows = gath[0]
        for i in range(1, NC):
            rows = rows + gath[i]
        m_z[pl.ds(z, 1)] = rows.reshape(1, 8, 128)
        for i in ZS:
            remote(m_z.at[z], m_z.at[z], gb_send.at[0], gb_recv.at[0], dev(x, y, z + i, core)).start()

    def heads_along_x():
        settle(gath_head.at[pl.ds(0, NC - 1)], gh_recv.at[0])
        for i in range(NC):
            a_x[x, PLACE[i] * 8 : (PLACE[i] + 1) * 8, :] = gath_head[i]
        for i in (2, 1, 3):
            remote(a_x.at[x], a_x.at[x], ax_send.at[0], ax_recv.at[0], dev(x + i, y, z, core)).start()

    def inv_along_x():
        settle(m_z.at[pl.ds(0, NZ - 1)], gb_recv.at[0])
        for j in range(4):
            m_x[x, j * 8 : (j + 1) * 8, :] = m_z[2 * j] + m_z[2 * j + 1]
        for i in (2, 1, 3):
            remote(m_x.at[x], m_x.at[x], gc_send.at[0], gc_recv.at[0], dev(x + i, y, z, core)).start()

    def block(s, u):
        return data.at[s, pl.ds(pl.multiple_of(u * 16, 16), 16)]

    def have(s, u):
        settle(block(s, u), blk_recv.at[s, u])

    def share(s, u, dz):
        remote(block(s, u), block(s, u), ag_send.at[0], blk_recv.at[s, u], dev(x, y, z + dz + NZ, core)).start()

    mine_u = lax.div(y, 2)
    lean_y = jnp.where(lax.rem(y, 2) == 0, 3, 1)
    subs = [mine_u, lax.rem(mine_u + lean_y, 4), lax.rem(mine_u + 4 - lean_y, 4), lax.rem(mine_u + 2, 4)]
    below = lax.rem(z + NZ - 2, NZ)
    above = lax.rem(z + 2, NZ)

    def give(i):
        have(z, subs[i])
        for dz in (1, -1, 2, -2):
            share(z, subs[i], dz)

    def pass_on(i):
        have(below, subs[i])
        for dz in (2, 1) if i in (0, 3) else (1,):
            share(below, subs[i], dz)
        have(above, subs[i])
        for dz in (-2, -1) if i in (1, 2) else (-1,):
            share(above, subs[i], dz)

    def weights():
        settle(a_x.at[pl.ds(0, 3)], ax_recv.at[0])
        heads = (a_x[0] + a_x[1] + a_x[2] + a_x[3]).T
        settle(m_x.at[pl.ds(0, 3)], gc_recv.at[0])
        inverse = m_x[...].reshape(NB, NB)
        gram = jnp.dot(inverse.T, inverse, precision=lax.Precision.HIGHEST, preferred_element_type=F32)
        w = jnp.dot(heads, gram, precision=lax.Precision.HIGHEST, preferred_element_type=F32)
        wh = w.astype(BF16)
        wcat[0:NB] = wh
        wcat[NB:] = (w - wh.astype(F32)).astype(BF16)

    mine_q = lax.div(z, 2)
    lean = jnp.where(lax.rem(z, 2) == 0, 3, 1)
    chunks = [mine_q, lax.rem(mine_q + lean, NQ), lax.rem(mine_q + 4 - lean, NQ), lax.rem(mine_q + 2, NQ)]
    exchange = []

    def chunk(n):
        q = chunks[n]
        for half in range(2):
            s = 2 * q + half

            @pl.when((s != z) & (s != below) & (s != above))
            def _():
                for u in range(4):
                    have(s, u)

        a = jnp.concatenate([data[2 * q], data[2 * q + 1]], axis=0)
        ah = a.astype(BF16)
        al = (a - ah.astype(F32)).astype(BF16)
        both = jnp.dot(wcat[...], ah, preferred_element_type=F32)
        outb[n] = both[0:NB] + both[NB:] + jnp.dot(wcat[0:NB], al, preferred_element_type=F32)
        for i in (2, 1, 3):
            other = lax.rem(x + i, NX)
            cp = remote(
                outb.at[n, pl.ds(pl.multiple_of(other * 32, 32), 32)],
                urecv.at[member, core, n],
                ex_send.at[i, n],
                ex_recv.at[member, core, n],
                dev(x + i, y, z, to_core),
            )
            cp.start()
            exchange.append(cp)
        own = outb.at[n, pl.ds(pl.multiple_of(x * 32, 32), 32)]

        @pl.when(to_core == core)
        def _():
            pltpu.make_async_copy(own, urecv.at[member, core, n], ex_recv.at[member, core, n]).start()

        @pl.when(to_core != core)
        def _():
            remote(
                own, urecv.at[member, core, n], ex_send.at[0, n], ex_recv.at[member, core, n], dev(x, y, z, 1 - core)
            ).start()

    steps = {"h": hop, "a": inv_along_z, "H": heads_along_x, "b": inv_along_x, "A": give, "B": pass_on, "W": weights, "C": chunk}
    for step in ORDER:
        steps[step[0]](*map(int, step[1:]))

    settle(stage.at[pl.ds(0, 3)], za_send.at[0])

    @pl.when(jnp.logical_not(active))
    def _():
        settle(stage.at[0], za_send.at[0])

    @pl.when(active)
    def _():
        settle(stage.at[pl.ds(0, NZ - 1)], sc_send.at[0])
        settle(panel_t.at[0, :, pl.ds(0, CW)], sc_send.at[0])

    @pl.when(active & (member == 1))
    def _():
        settle(panel_t.at[0, :, pl.ds(0, CW)], sc_send.at[0])

    settle(data.at[pl.ds(0, 7)], ag_send.at[0])

    settle(gath.at[pl.ds(0, NC - 1)], ga_send.at[0])
    settle(gath_head.at[pl.ds(0, NC - 1)], gh_send.at[0])
    settle(m_z.at[pl.ds(0, NZ - 1)], gb_send.at[0])
    settle(m_x.at[pl.ds(0, 3)], gc_send.at[0])
    settle(a_x.at[pl.ds(0, 3)], ax_send.at[0])

    even = lax.rem(lane, 2) == 0
    swap = lane + 1 - 2 * lax.rem(lane, 2)
    for n, q in enumerate(chunks):
        for h in range(2):
            for m in range(2):
                settle(urecv.at[m, h, n], ex_recv.at[m, h, n])
            for t in range(CW // 128):
                b = 24 * h + 2 * (q * (CW // 128) + t)
                for g in range(4):
                    u0 = urecv[0, h, n, g * 8 : (g + 1) * 8, t * 128 : (t + 1) * 128]
                    u1 = urecv[1, h, n, g * 8 : (g + 1) * 8, t * 128 : (t + 1) * 128]
                    low = jnp.where(even, u0, u1)
                    high = jnp.take_along_axis(jnp.where(even, u1, u0), swap, axis=1)
                    s0 = slab_t[g * 8 : (g + 1) * 8, pl.ds(pl.multiple_of(b * 128, 128), 128)]
                    s1 = slab_t[g * 8 : (g + 1) * 8, pl.ds(pl.multiple_of(b * 128 + 128, 128), 128)]
                    out_ref[pl.ds(g * 8 * 48 + b, 8, stride=48), :] = s0 - low
                    out_ref[pl.ds(g * 8 * 48 + b + 1, 8, stride=48), :] = s1 - high

        for cp in exchange[3 * n : 3 * n + 3]:
            cp.wait_send()

        @pl.when(to_core != core)
        def _():
            settle(outb.at[n, pl.ds(0, 32)], ex_send.at[0, n])


def body(inv_diag, panel, slab):
    dma = pltpu.SemaphoreType.DMA
    out = pl.pallas_call(
        kernel,
        out_shape=jax.ShapeDtypeStruct((1536, 128), F32),
        in_specs=[pl.BlockSpec(memory_space=pl.ANY)] * 3,
        out_specs=pl.BlockSpec(memory_space=pltpu.VMEM),
        scratch_shapes=[
            pltpu.VMEM((1, 4, 1, 8), F32),
            pltpu.VMEM((192, 128), F32),
            pltpu.VMEM((NQ, 8, 2 * CW), F32),
            pltpu.VMEM((1536, 128), F32),
            pltpu.VMEM((32, 6144), F32),
            pltpu.VMEM((8, 128), F32),
            pltpu.VMEM((8, 128), F32),
            pltpu.VMEM((NC, 8, 128), F32),
            pltpu.VMEM((NC, 8, 128), F32),
            pltpu.VMEM((NZ, 8, 128), F32),
            pltpu.VMEM((NX, 32, 128), F32),
            pltpu.VMEM((NX, NB, 128), F32),
            pltpu.VMEM((NZ, 8, 2 * CW), F32),
            pltpu.VMEM((NZ, NB // 2, CW), F32),
            pltpu.VMEM((NQ, NB, CW), F32),
            pltpu.VMEM((2, 2, NQ, 32, CW), F32),
            pltpu.VMEM((2 * NB, NB), BF16),
            dma((3,)),
            dma((1,)),
            dma((1,)),
            dma((1,)),
            dma((1,)),
            dma((1,)),
            dma((1,)),
            dma((1,)),
            dma((1,)),
            dma((1,)),
            dma((1,)),
            dma((1,)),
            dma((NZ,)),
            dma((1,)),
            dma((NZ, 4)),
            dma((1,)),
            dma((NX, NQ)),
            dma((2, 2, NQ)),
        ],
        compiler_params=pltpu.CompilerParams(
            collective_id=0, has_side_effects=True, vmem_limit_bytes=55_260_000
        ),
        cost_estimate=pl.CostEstimate(flops=200_000_000, bytes_accessed=1_700_000, transcendentals=0),
        name="panel_step",
    )(inv_diag, panel.reshape(192, 128), slab.reshape(1536, 128))
    return out.reshape(slab.shape)


def solution(mesh):
    return jax.shard_map(
        body,
        mesh=mesh,
        in_specs=(
            P("row", None, "col", None),
            P("col", None, "row", None),
            P("row", None, "col", None),
        ),
        out_specs=P("row", None, "col", None),
        check_vma=False,
    )
```

time: 48.7 us -> 47.7 us (0.979)
  Pallas kernels: 46.1 us -> 45 us
    pallas_call x1, Pallas kernels: 46.1 us -> 45 us  [body(): pl.pallas_call(kernel, out_shape=jax.ShapeDtypeStruct((1536, 128), F32),...]
    unnamed x1 -> x5, local copies, waits for them, and re-layouts: 2.06 us -> 2.46 us
where the time goes in v4:
time: 47.7 us; the launch traced here: 47.5 us
  Pallas kernels  45 us (94%)
  local copies, waits for them, and re-layouts  2.46 us (5%)
    pallas_call x1, Pallas kernels, body(): pl.pallas_call(kernel, out_shape=jax.ShapeDtypeStruct((1536, 128), F32),...  45 us
    unnamed x5, local copies, waits for them, and re-layouts  2.46 us

profile of v4, /device:TPU:1, one launch (start us, length us, event | category | flops | bytes accessed | tf_op | source)
XLA Modules:
  0.0 47.5 jit_solution(9471593995495750836)
XLA Ops:
  0.0 0.0 copy-start.1
  0.0 0.7 %copy-done.1 = f32[1,4,1,8]{3,2,1,0:T(1,128)S(1)} copy-done((f32[1,4,1,8]{3,2,1,0:T(1,128)S(1)}, f32[1,4,1,8]{3,2,1,0:T(1,128)}, u32[]{:S(2)}) %copy-start.1) | copy-done | bytes 152
  0.7 0.0 copy-start
  0.7 0.9 %copy-done = f32[1,8,1,3072]{3,2,1,0:T(1,128)S(1)} copy-done((f32[1,8,1,3072]{3,2,1,0:T(1,128)S(1)}, f32[1,8,1,3072]{3,2,1,0:T(1,128)}, u32[]{:S(2)}) %copy-start) | copy-done | bytes 98328
  1.6 45.0 %panel_step.1 = f32[1536,128]{1,0:T(8,128)S(1)} custom-call(f32[1,4,1,8]{3,2,1,0:T(1,128)S(1)} %copy-done.1, f32[192,128]{1,0:T(8,128)S(1)} %bitcast.4, f32[1536,128]{1,0:T(8,128)} %bitcast.5), custom_call_target="tpu_custom_call" | custom-call | flops 200000000 | bytes 1700000 | tf_op jit(solution)/shard_map/panel_step/pallas_call | solution.py:347
  46.6 0.9 %copy.6 = f32[1,32,1,6144]{3,2,1,0:T(1,128)} copy(f32[1,32,1,6144]{3,2,1,0:T(1,128)S(1)} %bitcast.3) | data formatting | bytes 1572864
Async XLA Ops:
  0.0 0.7 %copy-start.1 = (f32[1,4,1,8]{3,2,1,0:T(1,128)S(1)}, f32[1,4,1,8]{3,2,1,0:T(1,128)}, u32[]{:S(2)}) copy-start(f32[1,4,1,8]{3,2,1,0:T(1,128)} %inv_ref.1) | copy-start | bytes 388
  0.7 0.9 %copy-start = (f32[1,8,1,3072]{3,2,1,0:T(1,128)S(1)}, f32[1,8,1,3072]{3,2,1,0:T(1,128)}, u32[]{:S(2)}) copy-start(f32[1,8,1,3072]{3,2,1,0:T(1,128)} %param.4) | copy-start | bytes 294916

commit v5 on v4

--- a/solution.py
+++ b/solution.py
@@ -18,8 +18,8 @@
 ZS = (4, 3, 5, 2, 6, 1, 7)
 PLACE = [c % 2 * 8 + c // 2 for c in range(NC)]
 ORDER = (
-    "h0", "h1", "h7", "h2", "h6", "h3", "h5", "a", "h4", "A0", "H", "A1",
-    "b", "A2", "A3", "B0", "W", "B1", "C0", "B2", "B3", "C1", "C2", "C3",
+    "h0", "h1", "h7", "h2", "h6", "h3", "h5", "a", "h4", "H",
+    "A0", "b", "A1", "B0", "W", "C0", "B1", "C1", "C2", "C3",
 )
 
 
@@ -113,8 +113,7 @@
     for i in COLS:
         hello((row, lax.rem(col + i, NC)))
     for i in (2, 1, 3):
-        for k in range(2):
-            hello(dev(x + i, y, z, k))
+        hello(dev(x + i, y, z, core))
 
     lane = lax.broadcasted_iota(jnp.int32, (8, 128), 1)
     mine[...] = jnp.zeros_like(mine)
@@ -135,7 +134,7 @@
                 tile = panel_lin[pl.ds(12 * h + 3 * q + t, 8, stride=24), :]
                 panel_t[q, :, (3 * h + t) * 128 : (3 * h + t + 1) * 128] = jnp.take_along_axis(tile, perm, axis=1)
 
-    pl.semaphore_wait(barrier, (NC - 1) + (NZ - 1) + 2 * (NX - 1) + jnp.where(active, 8, 0))
+    pl.semaphore_wait(barrier, (NC - 1) + (NZ - 1) + (NX - 1) + jnp.where(active, 8, 0))
 
     for near, far in ((0, 1), (2, -1), (-2, 3), (4, -3)):
         zq = lax.rem(z + jnp.where(active, near, far) + NZ, NZ)
@@ -168,7 +167,7 @@
         goes_x = jnp.where(src < 4, x, 3 - x)
         goes_y = 2 * lax.rem(src, 4) + lax.div(x, 2)
         at_home = (goes_x == x) & (goes_y == y)
-        arrive = blk_recv.at[z, lax.div(y, 2)]
+        arrive = blk_recv.at[z, lax.div(y, 4)]
 
         @pl.when(active)
         def _():
@@ -208,7 +207,7 @@
             remote(m_x.at[x], m_x.at[x], gc_send.at[0], gc_recv.at[0], dev(x + i, y, z, core)).start()
 
     def block(s, u):
-        return data.at[s, pl.ds(pl.multiple_of(u * 16, 16), 16)]
+        return data.at[s, pl.ds(pl.multiple_of(u * 32, 32), 32)]
 
     def have(s, u):
         settle(block(s, u), blk_recv.at[s, u])
@@ -216,9 +215,7 @@
     def share(s, u, dz):
         remote(block(s, u), block(s, u), ag_send.at[0], blk_recv.at[s, u], dev(x, y, z + dz + NZ, core)).start()
 
-    mine_u = lax.div(y, 2)
-    lean_y = jnp.where(lax.rem(y, 2) == 0, 3, 1)
-    subs = [mine_u, lax.rem(mine_u + lean_y, 4), lax.rem(mine_u + 4 - lean_y, 4), lax.rem(mine_u + 2, 4)]
+    subs = [lax.div(y, 4), 1 - lax.div(y, 4)]
     below = lax.rem(z + NZ - 2, NZ)
     above = lax.rem(z + 2, NZ)
 
@@ -229,10 +226,10 @@
 
     def pass_on(i):
         have(below, subs[i])
-        for dz in (2, 1) if i in (0, 3) else (1,):
+        for dz in (2, 1) if i == 0 else (1,):
             share(below, subs[i], dz)
         have(above, subs[i])
-        for dz in (-2, -1) if i in (1, 2) else (-1,):
+        for dz in (-2, -1) if i == 1 else (-1,):
             share(above, subs[i], dz)
 
     def weights():
@@ -258,7 +255,7 @@
 
             @pl.when((s != z) & (s != below) & (s != above))
             def _():
-                for u in range(4):
+                for u in range(2):
                     have(s, u)
 
         a = jnp.concatenate([data[2 * q], data[2 * q + 1]], axis=0)
@@ -381,7 +378,7 @@
             dma((1,)),
             dma((NZ,)),
             dma((1,)),
-            dma((NZ, 4)),
+            dma((NZ, 2)),
             dma((1,)),
             dma((NX, NQ)),
             dma((2, 2, NQ)),

time: 47.7 us -> 47.5 us (level)
  no operation moved by 1% of the time
where the time goes in v5:
time: 47.5 us; the launch traced here: 47.3 us
  Pallas kernels  44.8 us (94%)
  local copies, waits for them, and re-layouts  2.46 us (5%)
    pallas_call x1, Pallas kernels, body(): pl.pallas_call(kernel, out_shape=jax.ShapeDtypeStruct((1536, 128), F32),...  44.8 us
    unnamed x5, local copies, waits for them, and re-layouts  2.46 us

profile of v5, /device:TPU:1, one launch (start us, length us, event | category | flops | bytes accessed | tf_op | source)
XLA Modules:
  0.0 47.3 jit_solution(18374317062695756824)
XLA Ops:
  0.0 0.0 copy-start.1
  0.0 0.7 %copy-done.1 = f32[1,4,1,8]{3,2,1,0:T(1,128)S(1)} copy-done((f32[1,4,1,8]{3,2,1,0:T(1,128)S(1)}, f32[1,4,1,8]{3,2,1,0:T(1,128)}, u32[]{:S(2)}) %copy-start.1) | copy-done | bytes 152
  0.7 0.0 copy-start
  0.7 0.9 %copy-done = f32[1,8,1,3072]{3,2,1,0:T(1,128)S(1)} copy-done((f32[1,8,1,3072]{3,2,1,0:T(1,128)S(1)}, f32[1,8,1,3072]{3,2,1,0:T(1,128)}, u32[]{:S(2)}) %copy-start) | copy-done | bytes 98328
  1.6 44.8 %panel_step.1 = f32[1536,128]{1,0:T(8,128)S(1)} custom-call(f32[1,4,1,8]{3,2,1,0:T(1,128)S(1)} %copy-done.1, f32[192,128]{1,0:T(8,128)S(1)} %bitcast.4, f32[1536,128]{1,0:T(8,128)} %bitcast.5), custom_call_target="tpu_custom_call" | custom-call | flops 200000000 | bytes 1700000 | tf_op jit(solution)/shard_map/panel_step/pallas_call | solution.py:344
  46.4 0.9 %copy.6 = f32[1,32,1,6144]{3,2,1,0:T(1,128)} copy(f32[1,32,1,6144]{3,2,1,0:T(1,128)S(1)} %bitcast.3) | data formatting | bytes 1572864
Async XLA Ops:
  0.0 0.7 %copy-start.1 = (f32[1,4,1,8]{3,2,1,0:T(1,128)S(1)}, f32[1,4,1,8]{3,2,1,0:T(1,128)}, u32[]{:S(2)}) copy-start(f32[1,4,1,8]{3,2,1,0:T(1,128)} %inv_ref.1) | copy-start | bytes 388
  0.7 0.9 %copy-start = (f32[1,8,1,3072]{3,2,1,0:T(1,128)S(1)}, f32[1,8,1,3072]{3,2,1,0:T(1,128)}, u32[]{:S(2)}) copy-start(f32[1,8,1,3072]{3,2,1,0:T(1,128)} %param.4) | copy-start | bytes 294916

commit v6 on v5

--- a/solution.py
+++ b/solution.py
@@ -28,8 +28,6 @@
     panel_ref,
     slab_ref,
     out_ref,
-    inv_v,
-    panel_lin,
     panel_t,
     slab_lin,
     slab_t,
@@ -90,9 +88,7 @@
     active = core == lax.rem(z, 2)
 
     loads = [
-        pltpu.make_async_copy(inv_ref, inv_v, in_sem.at[0]),
-        pltpu.make_async_copy(panel_ref, panel_lin, in_sem.at[1]),
-        pltpu.make_async_copy(slab_ref, slab_lin, in_sem.at[2]),
+        pltpu.make_async_copy(slab_ref, slab_lin, in_sem.at[0]),
     ]
     for load in loads:
         load.start()
@@ -117,13 +113,11 @@
 
     lane = lax.broadcasted_iota(jnp.int32, (8, 128), 1)
     mine[...] = jnp.zeros_like(mine)
-    loads[0].wait()
     for i in range(4):
-        mine[i : i + 1, 0:8] = inv_v[0, i, :, :]
+        mine[i : i + 1, 0:8] = inv_ref[0, i, :, :]
     placed = pltpu.roll(pltpu.roll(mine[...], (core * 8 + y) * 8, 1), 4 * lax.rem(z, 2), 0)
     mine[...] = placed
-    loads[1].wait()
-    head = panel_lin[pl.ds(0, 8, stride=24), :]
+    head = panel_ref[pl.ds(0, 8, stride=24), :]
     mine_head[...] = pltpu.roll(jnp.where(lane < 32, head, 0.0), x * 32, 1)
     gath_head[pl.ds(col, 1)] = mine_head[...].reshape(1, 8, 128)
     gath[pl.ds(col, 1)] = mine[...].reshape(1, 8, 128)
@@ -131,7 +125,7 @@
     for q in range(NQ):
         for h in range(2):
             for t in range(3):
-                tile = panel_lin[pl.ds(12 * h + 3 * q + t, 8, stride=24), :]
+                tile = panel_ref[pl.ds(12 * h + 3 * q + t, 8, stride=24), :]
                 panel_t[q, :, (3 * h + t) * 128 : (3 * h + t + 1) * 128] = jnp.take_along_axis(tile, perm, axis=1)
 
     pl.semaphore_wait(barrier, (NC - 1) + (NZ - 1) + (NX - 1) + jnp.where(active, 8, 0))
@@ -155,7 +149,7 @@
             mine_head, gath_head.at[col], gh_send.at[0], gh_recv.at[0], (row, lax.rem(col + i, NC))
         ).start()
 
-    loads[2].wait()
+    loads[0].wait()
     for g in range(4):
         for b in range(48):
             slab_t[g * 8 : (g + 1) * 8, b * 128 : (b + 1) * 128] = slab_lin[pl.ds(g * 8 * 48 + b, 8, stride=48), :]
@@ -344,11 +338,9 @@
     out = pl.pallas_call(
         kernel,
         out_shape=jax.ShapeDtypeStruct((1536, 128), F32),
-        in_specs=[pl.BlockSpec(memory_space=pl.ANY)] * 3,
+        in_specs=[pl.BlockSpec(memory_space=pltpu.VMEM)] * 2 + [pl.BlockSpec(memory_space=pl.ANY)],
         out_specs=pl.BlockSpec(memory_space=pltpu.VMEM),
         scratch_shapes=[
-            pltpu.VMEM((1, 4, 1, 8), F32),
-            pltpu.VMEM((192, 128), F32),
             pltpu.VMEM((NQ, 8, 2 * CW), F32),
             pltpu.VMEM((1536, 128), F32),
             pltpu.VMEM((32, 6144), F32),
@@ -364,7 +356,7 @@
             pltpu.VMEM((NQ, NB, CW), F32),
             pltpu.VMEM((2, 2, NQ, 32, CW), F32),
             pltpu.VMEM((2 * NB, NB), BF16),
-            dma((3,)),
+            dma((1,)),
             dma((1,)),
             dma((1,)),
             dma((1,)),

time: 47.5 us -> 47.3 us (level)
  no operation moved by 1% of the time
where the time goes in v6:
time: 47.3 us; the launch traced here: 47.1 us
  Pallas kernels  44.7 us (95%)
  local copies, waits for them, and re-layouts  2.46 us (5%)
    pallas_call x1, Pallas kernels, body(): pl.pallas_call(kernel, out_shape=jax.ShapeDtypeStruct((1536, 128), F32),...  44.7 us
    unnamed x5, local copies, waits for them, and re-layouts  2.46 us

profile of v6, /device:TPU:1, one launch (start us, length us, event | category | flops | bytes accessed | tf_op | source)
XLA Modules:
  0.0 47.1 jit_solution(9777735010007053314)
XLA Ops:
  0.0 0.0 copy-start.1
  0.0 0.7 %copy-done.1 = f32[1,4,1,8]{3,2,1,0:T(1,128)S(1)} copy-done((f32[1,4,1,8]{3,2,1,0:T(1,128)S(1)}, f32[1,4,1,8]{3,2,1,0:T(1,128)}, u32[]{:S(2)}) %copy-start.1) | copy-done | bytes 152
  0.7 0.0 copy-start
  0.7 0.9 %copy-done = f32[1,8,1,3072]{3,2,1,0:T(1,128)S(1)} copy-done((f32[1,8,1,3072]{3,2,1,0:T(1,128)S(1)}, f32[1,8,1,3072]{3,2,1,0:T(1,128)}, u32[]{:S(2)}) %copy-start) | copy-done | bytes 98328
  1.6 44.7 %panel_step.1 = f32[1536,128]{1,0:T(8,128)S(1)} custom-call(f32[1,4,1,8]{3,2,1,0:T(1,128)S(1)} %copy-done.1, f32[192,128]{1,0:T(8,128)S(1)} %bitcast.4, f32[1536,128]{1,0:T(8,128)} %bitcast.5), custom_call_target="tpu_custom_call" | custom-call | flops 200000000 | bytes 1700000 | tf_op jit(solution)/shard_map/panel_step/pallas_call | solution.py:338
  46.2 0.9 %copy.6 = f32[1,32,1,6144]{3,2,1,0:T(1,128)} copy(f32[1,32,1,6144]{3,2,1,0:T(1,128)S(1)} %bitcast.3) | data formatting | bytes 1572864
Async XLA Ops:
  0.0 0.7 %copy-start.1 = (f32[1,4,1,8]{3,2,1,0:T(1,128)S(1)}, f32[1,4,1,8]{3,2,1,0:T(1,128)}, u32[]{:S(2)}) copy-start(f32[1,4,1,8]{3,2,1,0:T(1,128)} %inv_ref.1) | copy-start | bytes 388
  0.7 0.9 %copy-start = (f32[1,8,1,3072]{3,2,1,0:T(1,128)S(1)}, f32[1,8,1,3072]{3,2,1,0:T(1,128)}, u32[]{:S(2)}) copy-start(f32[1,8,1,3072]{3,2,1,0:T(1,128)} %param.4) | copy-start | bytes 294916

commit v7 on v6

--- a/solution.py
+++ b/solution.py
@@ -18,7 +18,7 @@
 ZS = (4, 3, 5, 2, 6, 1, 7)
 PLACE = [c % 2 * 8 + c // 2 for c in range(NC)]
 ORDER = (
-    "h0", "h1", "h7", "h2", "h6", "h3", "h5", "a", "h4", "H",
+    "h0", "h1", "h7", "E", "h2", "h6", "h3", "h5", "a", "h4", "H",
     "A0", "b", "A1", "B0", "W", "C0", "B1", "C1", "C2", "C3",
 )
 
@@ -144,10 +144,6 @@
 
     for i in COLS:
         remote(mine, gath.at[col], ga_send.at[0], ga_recv.at[0], (row, lax.rem(col + i, NC))).start()
-    for i in COLS:
-        remote(
-            mine_head, gath_head.at[col], gh_send.at[0], gh_recv.at[0], (row, lax.rem(col + i, NC))
-        ).start()
 
     loads[0].wait()
     for g in range(4):
@@ -280,7 +276,13 @@
                 own, urecv.at[member, core, n], ex_send.at[0, n], ex_recv.at[member, core, n], dev(x, y, z, 1 - core)
             ).start()
 
-    steps = {"h": hop, "a": inv_along_z, "H": heads_along_x, "b": inv_along_x, "A": give, "B": pass_on, "W": weights, "C": chunk}
+    def send_heads():
+        for i in COLS:
+            remote(
+                mine_head, gath_head.at[col], gh_send.at[0], gh_recv.at[0], (row, lax.rem(col + i, NC))
+            ).start()
+
+    steps = {"E": send_heads, "h": hop, "a": inv_along_z, "H": heads_along_x, "b": inv_along_x, "A": give, "B": pass_on, "W": weights, "C": chunk}
     for step in ORDER:
         steps[step[0]](*map(int, step[1:]))
 

time: 47.3 us -> 47 us (level); the launches traced: 47.1 us -> 46.2 us
  Pallas kernels: 44.7 us -> 43.8 us
    pallas_call x1, Pallas kernels: 44.7 us -> 43.8 us  [body(): pl.pallas_call(kernel, out_shape=jax.ShapeDtypeStruct((1536, 128), F32),...]
where the time goes in v7:
time: 47 us; the launch traced here: 46.2 us
  Pallas kernels  43.8 us (93%)
  local copies, waits for them, and re-layouts  2.46 us (5%)
    pallas_call x1, Pallas kernels, body(): pl.pallas_call(kernel, out_shape=jax.ShapeDtypeStruct((1536, 128), F32),...  43.8 us
    unnamed x5, local copies, waits for them, and re-layouts  2.46 us

profile of v7, /device:TPU:1, one launch (start us, length us, event | category | flops | bytes accessed | tf_op | source)
XLA Modules:
  0.0 46.2 jit_solution(6978172465589975242)
XLA Ops:
  0.0 0.0 copy-start.1
  0.0 0.7 %copy-done.1 = f32[1,4,1,8]{3,2,1,0:T(1,128)S(1)} copy-done((f32[1,4,1,8]{3,2,1,0:T(1,128)S(1)}, f32[1,4,1,8]{3,2,1,0:T(1,128)}, u32[]{:S(2)}) %copy-start.1) | copy-done | bytes 152
  0.7 0.0 copy-start
  0.7 0.9 %copy-done = f32[1,8,1,3072]{3,2,1,0:T(1,128)S(1)} copy-done((f32[1,8,1,3072]{3,2,1,0:T(1,128)S(1)}, f32[1,8,1,3072]{3,2,1,0:T(1,128)}, u32[]{:S(2)}) %copy-start) | copy-done | bytes 98328
  1.6 43.8 %panel_step.1 = f32[1536,128]{1,0:T(8,128)S(1)} custom-call(f32[1,4,1,8]{3,2,1,0:T(1,128)S(1)} %copy-done.1, f32[192,128]{1,0:T(8,128)S(1)} %bitcast.4, f32[1536,128]{1,0:T(8,128)} %bitcast.5), custom_call_target="tpu_custom_call" | custom-call | flops 200000000 | bytes 1700000 | tf_op jit(solution)/shard_map/panel_step/pallas_call | solution.py:340
  45.4 0.9 %copy.6 = f32[1,32,1,6144]{3,2,1,0:T(1,128)} copy(f32[1,32,1,6144]{3,2,1,0:T(1,128)S(1)} %bitcast.3) | data formatting | bytes 1572864
Async XLA Ops:
  0.0 0.7 %copy-start.1 = (f32[1,4,1,8]{3,2,1,0:T(1,128)S(1)}, f32[1,4,1,8]{3,2,1,0:T(1,128)}, u32[]{:S(2)}) copy-start(f32[1,4,1,8]{3,2,1,0:T(1,128)} %inv_ref.1) | copy-start | bytes 388
  0.7 0.9 %copy-start = (f32[1,8,1,3072]{3,2,1,0:T(1,128)S(1)}, f32[1,8,1,3072]{3,2,1,0:T(1,128)}, u32[]{:S(2)}) copy-start(f32[1,8,1,3072]{3,2,1,0:T(1,128)} %param.4) | copy-start | bytes 294916
